TPU v7x, 256 devices: a whole 4x4x8 slice. The times are simulated.
256 devices in a mesh: row: 16 (over x, z_lo, core), col: 16 (over z_hi, y).
Axes of the slice: x: 4, y: 4, z: 8 (z_hi: 4, z_lo: 2; z = z_hi * 2 + z_lo), core: 2. Of those that a mesh axis runs over, the one named last changes fastest.
Arguments:
- jacobian: bfloat16 [16, 16, 56, 320, 320], P('row', 'col'), may hold values from -3 to 3
- prolong: bfloat16 [2048, 64, 320], P(('row', 'col')), may hold values from -0.3125 to 0.3125
- tile_rows: int32 [16, 16, 56], P('row', 'col'), may hold values from 0 to 127, as said below
- tile_cols: int32 [16, 16, 56], P('row', 'col'), may hold values from 0 to 127
- coarse_slot: int32 [16, 16, 56], P('row', 'col'), may hold values from 0 to 1
Outputs:
- coarse: float32 [16, 16, 64, 128], P('row', 'col')
Inputs may be any that keep to these rules, and one draw needn't show every extreme that they name: On every device at most 5 tiles have tile_rows // 8 equal to one value, and exactly 5 for some value.
All inputs are finite; a program needn't handle non-finite values.
Results may differ from a plain program's by a relative error of at most 0.0029.
Values may be sent and summed in bfloat16 or wider, within the bound.
A program may use at most 64 MiB of HBM per device.

v0:
```python
import jax
import jax.numpy as jnp
from jax import lax
from jax.sharding import PartitionSpec as P

CT_DEV = 2


def per_device(jacobian, prolong, tile_rows, tile_cols, coarse_slot):
    blocks = prolong.shape[0]
    width = prolong.shape[1]
    col_count = lax.axis_size("col")
    tiles = jacobian[0, 0]
    rows = tile_rows[0, 0]
    cols = tile_cols[0, 0]
    slots = coarse_slot[0, 0]
    owned = CT_DEV
    col_side = lax.all_gather(prolong, "row", axis=0, tiled=True)
    picked = jnp.take(col_side, cols, axis=0)
    images = jnp.einsum("kab,kcb->kca", tiles, picked, preferred_element_type=jnp.float32).astype(
        jnp.bfloat16
    )
    row_side = lax.all_gather(prolong, "col", axis=0, tiled=True)
    left = jnp.take(row_side, rows, axis=0)
    parts = jnp.einsum("kct,kdt->kcd", left, images, preferred_element_type=jnp.float32)
    target = rows // blocks * owned + slots
    onehot = (target[:, None] == jnp.arange(col_count * owned, dtype=jnp.int32)[None, :]).astype(
        jnp.float32
    )
    term = jnp.einsum("kn,kcd->ncd", onehot, parts, precision=lax.Precision.HIGHEST)
    term = term.reshape(col_count, owned, width, width).transpose(0, 2, 1, 3)
    term = term.reshape(col_count, width, owned * width)
    result = lax.psum_scatter(term, "col", scatter_dimension=0, tiled=True)
    return result.reshape(1, 1, width, owned * width)


def solution(mesh):
    placed = (
        P("row", "col", None, None, None),
        P(("row", "col"), None, None),
        P("row", "col", None),
        P("row", "col", None),
        P("row", "col", None),
    )
    return jax.shard_map(
        per_device,
        mesh=mesh,
        in_specs=placed,
        out_specs=P("row", "col", None, None),
        check_vma=False,
    )
```

profile of v0, /device:TPU:1, one launch (start us, length us, event | category | flops | bytes accessed | tf_op | source)
XLA Modules:
  0.0 267.3 jit_solution(4885913590338577221)
XLA Ops:
  6.5 0.0 all-gather.3.cloned.1.call-start
  6.5 0.7 all-gather.3.cloned.1.call-update
  7.3 0.0 all-gather.5.cloned.1.call-start
  7.3 0.7 all-gather.5.cloned.1.call-update
  8.0 0.0 reduce-scatter.2.cloned.1.call-start
  8.1 0.7 bitcast_add_fusion
  8.7 0.7 compare_select_fusion
  9.4 0.7 compare_and_fusion
  10.1 94.3 %all-gather.3.cloned.1.call-done = bf16[128,64,320]{2,1,0:T(8,128)(2,1)} async-done(((bf16[8,64,320]{2,1,0:T(8,128)(2,1)}), bf16[128,64,320]{2,1,0:T(8,128)(2,1)}) %all-gather.3.cloned.1.call-update) | async-done | bytes 5242896 | tf_op jit(solution)/shard_map/all_gather | solution.py:23
  104.4 4.0 %gather_fusion = bf16[56,64,320]{2,1,0:T(8,128)(2,1)S(1)} fusion(bf16[128,64,320]{2,1,0:T(8,128)(2,1)} %all-gather.3.cloned.1.call-done, s32[1024]{0:T(1024)S(1)} %pad_clamp_fusion.1), kind=kCustom, calls=%fused_computation.clone | custom fusion | bytes 4587744 | tf_op jit(solution)/shard_map/jit(_take)/gather | solution.py:24
  108.4 48.0 %all-gather.5.cloned.1.call-done = bf16[128,64,320]{2,1,0:T(8,128)(2,1)} async-done(((bf16[8,64,320]{2,1,0:T(8,128)(2,1)}), bf16[128,64,320]{2,1,0:T(8,128)(2,1)}) %all-gather.5.cloned.1.call-update) | async-done | bytes 5242896 | tf_op jit(solution)/shard_map/all_gather | solution.py:18
  156.4 5.4 %gather_fusion.1 = bf16[56,64,320]{2,1,0:T(8,128)(2,1)} fusion(bf16[128,64,320]{2,1,0:T(8,128)(2,1)} %all-gather.5.cloned.1.call-done, s32[1024]{0:T(1024)S(1)} %pad_clamp_fusion), kind=kCustom, calls=%fused_computation.1.clone | custom fusion | bytes 4587744 | tf_op jit(solution)/shard_map/jit(_take)/gather | solution.py:19
  161.9 9.7 %fusion.3 = f32[56,64,64]{2,1,0:T(8,128)} fusion(bf16[56,64,320]{2,1,0:T(8,128)(2,1)S(1)} %gather_fusion, pred[56]{0:T(512)(128)(4,1)S(1)} %get-tuple-element.9, bf16[1,1,56,320,320]{4,3,2,1,0:T(8,128)(2,1)} %param.7, bf16[56,64,320]{2,1,0:T(8,128)(2,1)} %gather_fusion.1, pred[56]{0:T(512)(128)(4,1)S(1)} %get-tuple-element.8), kind=kOutput, calls=%fused_computation.5 | convolution fusion | flops 884244480 | bytes 16973936 | tf_op jit(solution)/shard_map/kct,kdt->kcd/dot_general | solution.py:25
  171.6 3.3 %fusion.16 = f32[32,64,64]{2,0,1:T(8,128)S(1)} fusion(f32[56,64,64]{2,1,0:T(8,128)} %fusion.3, s32[56]{0:T(128)S(1)} %get-tuple-element.6), kind=kOutput, calls=%fused_computation.10 | convolution fusion | flops 88082176 | bytes 1442016 | tf_op jit(solution)/shard_map/kn,kcd->ncd/dot_general | solution.py:30
  174.9 0.6 reshape.74
  175.5 1.0 copy.9
  176.5 0.0 reduce-scatter.2.cloned.1.call-update
  176.5 84.3 %reduce-scatter.2.cloned.1.call-done = f32[1,64,128]{2,1,0:T(8,128)} async-done(((f32[16,64,128]{2,1,0:T(8,128)}), f32[1,64,128]{2,1,0:T(8,128)}) %reduce-scatter.2.cloned.1.call-update) | async-done | bytes 32784 | tf_op jit(solution)/shard_map/reduce_scatter | solution.py:33
  (2 shorter events, 0.0 us)
Async XLA Ops:
  6.5 97.9 %all-gather.3.cloned.1.call-start = ((), (), s32[]{:S(2)}) async-start(), calls=%async_computation.1 | async-start | bytes 6684672 | tf_op jit(solution)/shard_map/all_gather | solution.py:23
  7.3 149.2 %all-gather.5.cloned.1.call-start = ((), (), s32[]{:S(2)}) async-start(), calls=%async_computation.2 | async-start | bytes 6684672 | tf_op jit(solution)/shard_map/all_gather | solution.py:18
  8.0 252.8 %reduce-scatter.2.cloned.1.call-start = ((), (), s32[]{:S(2)}) async-start(), calls=%async_computation.3 | async-start | bytes 557056 | tf_op jit(solution)/shard_map/reduce_scatter | solution.py:33
Sparse Core Ops, SparseCore 0:
  9.8 94.5 all-gather.2
  106.3 50.1 all-gather.4
  176.6 84.1 reduce-scatter.1
where the time goes:
time: 269 us; the launch traced here: 267 us
  waiting for transfers between devices  228 us (85%)
  matrix products  13.1 us (5%)
  between operations  13.1 us (5%)
  local copies, waits for them, and re-layouts  10.9 us (4%)
    all_gather x1, waiting for transfers between devices, per_device(): row_side = lax.all_gather(prolong, 'col', axis=0, tiled=True)  94.3 us
    reduce_scatter x1, waiting for transfers between devices, per_device(): result = lax.psum_scatter(term, 'col', scatter_dimension=0, tiled=True)  84.3 us
    all_gather x1, waiting for transfers between devices, per_device(): col_side = lax.all_gather(prolong, 'row', axis=0, tiled=True)  48 us
    dot_general x1, matrix products, per_device(): jnp.einsum('kct,kdt->kcd', left, images, preferred_element_type=jnp.float32)  9.74 us
    gather x1, local copies, waits for them, and re-layouts, per_device(): picked = jnp.take(col_side, cols, axis=0)  5.41 us
  transfers between devices with their start and end apart: 3, of which 3 were waited for; matrix products, arithmetic and copies ran while one was open for 2% of the time, Pallas kernels for 0%

commit v1 on v0

v1 whole, which is shorter than its diff:
```python
import functools

import jax
import jax.numpy as jnp
from jax import lax
from jax.experimental import pallas as pl
from jax.experimental.pallas import tpu as pltpu
from jax.sharding import PartitionSpec as P

MESH = pl.DeviceIdType.MESH
NX, NZL, NC, NZH, NY = 4, 2, 2, 4, 4
FB = 8
CAP = 5
PR, PC = 80, 256
HALF = FB // 2


def pack(p):
    t = p[:, 256:320]
    a = jnp.concatenate([t[0:16], t[16:32]], axis=1)
    b = jnp.concatenate([t[32:48], t[48:64]], axis=1)
    return jnp.concatenate([p[:, 0:256], jnp.concatenate([a, b], axis=1)], axis=0)


def unpack(v):
    q = v[64:80]
    tail = jnp.concatenate([q[:, 0:64], q[:, 64:128], q[:, 128:192], q[:, 192:256]], axis=0)
    return jnp.concatenate([v[0:64], tail], axis=1)


def kernel(
    jac, pro, rows, slots, cols, out,
    tiles, shard_in, colbuf, own, zm, zp, z2, picked, given, images, terms, landed,
    tab, tab_s, asked, asked_s, mask, local_sem, ask_sem, ss, rs,
):
    kt = tiles.shape[0]
    r = lax.axis_index("row")
    q = lax.axis_index("col")
    x, zl, c = r // 4, (r // 2) % 2, r % 2
    zh, y = q // NY, q % NY

    def dev(dx=0, dzl=0, dc=0, dzh=0, dy=0):
        return (
            ((x + dx) % NX) * 4 + ((zl + dzl) % NZL) * 2 + (c + dc) % NC,
            ((zh + dzh) % NZH) * NY + (y + dy) % NY,
        )

    def held(dx=0, dzl=0, dc=0):
        return (((x + dx) % NX) * 4 + ((zl + dzl) % NZL) * 2 + (c + dc) % NC) * FB

    sent = []
    count = [0]
    ids = {}

    def ident(name):
        if name not in ids:
            ids[name] = count[0]
            count[0] += 1
        return ids[name]

    def send(name, src, dst, to):
        i = ident(name)
        copy = pltpu.make_async_remote_copy(
            src_ref=src, dst_ref=dst, send_sem=ss.at[i], recv_sem=rs.at[i], device_id=to, device_id_type=MESH
        )
        copy.start()
        sent.append(copy)

    def arrive(name, dst):
        i = ident(name)
        pltpu.make_async_remote_copy(
            src_ref=dst, dst_ref=dst, send_sem=ss.at[i], recv_sem=rs.at[i], device_id=dev(dc=1), device_id_type=MESH
        ).wait_recv()

    get_tiles = pltpu.make_async_copy(jac, tiles, local_sem.at[0])
    get_shard = pltpu.make_async_copy(pro, shard_in, local_sem.at[1])
    get_shard.start()
    get_tiles.start()

    bar = pltpu.get_barrier_semaphore()
    peers = [dev(dc=1), dev(dzl=1), dev(dx=1), dev(dx=3)]
    peers += [dev(dzh=a, dy=b) for a in range(NZH) for b in range(NY) if (a, b) != (0, 0)]
    for peer in peers:
        pl.semaphore_signal(bar, inc=1, device_id=peer, device_id_type=MESH)

    row = rows[...]
    owner_row = jnp.right_shift(row, 3)
    block_row = jnp.bitwise_and(row, 7)
    sub = lax.broadcasted_iota(jnp.int32, (kt, kt), 0)
    lane = lax.broadcasted_iota(jnp.int32, (kt, kt), 1)
    diag = sub == lane
    owner_col = jnp.sum(jnp.where(diag, owner_row, 0), axis=1, keepdims=True)
    block_col = jnp.sum(jnp.where(diag, block_row, 0), axis=1, keepdims=True)
    same = owner_col == owner_row
    rank_col = jnp.sum(jnp.where(same & (lane < sub), 1, 0), axis=1, keepdims=True)
    rank_row = jnp.sum(jnp.where(same & (sub < lane), 1, 0), axis=0, keepdims=True)
    at_col = owner_col * 8 + rank_col
    at_row = owner_row * 8 + rank_row
    hot = at_col == lax.broadcasted_iota(jnp.int32, (kt, 128), 1)
    number = lax.broadcasted_iota(jnp.int32, (kt, 128), 0)
    tab[0:1, :] = jnp.sum(jnp.where(hot, number, 0), axis=0, keepdims=True)
    tab[1:2, :] = jnp.sum(jnp.where(hot, block_col, 0), axis=0, keepdims=True)
    tab[2:8, :] = jnp.zeros((6, 128), jnp.int32)
    put_tab = pltpu.make_async_copy(tab, tab_s, local_sem.at[2])
    put_tab.start()
    hot2 = at_row == lax.broadcasted_iota(jnp.int32, (128, kt), 0)
    which = jnp.sum(jnp.where(hot2, slots[...] + 1, 0), axis=1, keepdims=True)
    half = jnp.right_shift(lax.broadcasted_iota(jnp.int32, (128, 128), 1), 6) + 1
    mask[...] = jnp.where(half == which, 1.0, 0.0)

    get_shard.wait()
    mine = held()
    for b in range(FB):
        v = pack(shard_in[b])
        own[b] = v
        colbuf[mine + b] = v

    pl.semaphore_wait(bar, len(peers))

    def slot_of(at, first=0, n=FB):
        return colbuf.at[pl.ds(at + first, n)]

    for dy in range(1, NY):
        send(f"ask{dy}", tab, asked.at[dy - 1], dev(dy=dy))
    send("zl", own, slot_of(mine), dev(dzl=1))
    send("xp", own, slot_of(mine), dev(dx=1))
    send("xm", own, slot_of(mine), dev(dx=3))
    send("zp", own, zm, dev(dzh=1))
    send("zm", own, zp, dev(dzh=3))
    send("sib", own, slot_of(mine), dev(dc=1))

    put_tab.wait()
    asks = []
    for dy in range(1, NY):
        arrive(f"ask{dy}", asked.at[dy - 1])
        copy = pltpu.make_async_copy(asked.at[dy - 1], asked_s.at[dy - 1], ask_sem.at[dy - 1])
        copy.start()
        asks.append(copy)
    for copy in asks:
        copy.wait()

    def hand_out(dz, shard):
        owner = ((zh + dz) % NZH) * NY + y
        for d in (1, 3, 2):
            to = NY - d
            for j in range(CAP):
                picked[dz, to - 1, j] = shard[asked_s[d - 1, 1, owner * 8 + j]]
            send(f"y{dz}{to}", picked.at[dz, to - 1], given.at[dz, to - 1], dev(dy=to))

    hand_out(0, own)

    def across(tag, dzl):
        at = held(dx=3, dzl=dzl)
        arrive(f"xp{tag}", slot_of(at))
        send(f"xpp{tag}", slot_of(at, 0, HALF), slot_of(at, 0, HALF), dev(dx=1))
        send(f"sxp{tag}", slot_of(at), slot_of(at), dev(dc=1))
        at = held(dx=1, dzl=dzl)
        arrive(f"xm{tag}", slot_of(at))
        send(f"xmm{tag}", slot_of(at, HALF, HALF), slot_of(at, HALF, HALF), dev(dx=3))
        send(f"sxm{tag}", slot_of(at), slot_of(at), dev(dc=1))

    def beyond(tag, dzl):
        at = held(dx=2, dzl=dzl)
        arrive(f"xpp{tag}", slot_of(at, 0, HALF))
        arrive(f"xmm{tag}", slot_of(at, HALF, HALF))
        send(f"sx2{tag}", slot_of(at), slot_of(at), dev(dc=1))

    across("", 0)
    at = held(dzl=1)
    arrive("zl", slot_of(at))
    send("xp1", slot_of(at), slot_of(at), dev(dx=1))
    send("xm1", slot_of(at), slot_of(at), dev(dx=3))
    send("szl", slot_of(at), slot_of(at), dev(dc=1))
    beyond("", 0)

    arrive("zp", zm)
    send("zpp", zm.at[pl.ds(0, HALF)], z2.at[pl.ds(0, HALF)], dev(dzh=1))
    arrive("zm", zp)
    send("zmm", zp.at[pl.ds(HALF, HALF)], z2.at[pl.ds(HALF, HALF)], dev(dzh=3))
    hand_out(3, zm)
    hand_out(1, zp)

    across("1", 1)
    arrive("zpp", z2.at[pl.ds(0, HALF)])
    arrive("zmm", z2.at[pl.ds(HALF, HALF)])
    hand_out(2, z2)
    beyond("1", 1)

    at = held(dc=1)
    arrive("sib", slot_of(at))
    for tag, dzl in (("", 0), ("1", 1)):
        for name, dx in (("sxp", 3), ("sxm", 1), ("sx2", 2)):
            at = held(dx=dx, dzl=dzl, dc=1)
            arrive(name + tag, slot_of(at))
    at = held(dzl=1, dc=1)
    arrive("szl", slot_of(at))
    get_tiles.wait()

    def image(k, carry):
        p = unpack(colbuf[cols[0, k]])
        pp = jnp.concatenate([p, p], axis=0)
        images[k] = lax.dot_general(
            tiles[k], pp, (((1,), (1,)), ((), ())), preferred_element_type=jnp.float32
        ).astype(jnp.bfloat16)
        return carry

    lax.fori_loop(0, kt, image, 0, unroll=2)

    shards = {0: own, 1: zp, 2: z2, 3: zm}
    here = None
    for dz in (0, 3, 1, 2):
        for dy in (0, 1, 3, 2):
            o = ((zh + dz) % NZH) * NY + (y + dy) % NY
            if dy:
                arrive(f"y{dz}{NY - dy}", given.at[dz, NY - dy - 1])
            m = mask[pl.ds(pl.multiple_of(o * 8, 8), 8), :]
            total = None
            for j in range(CAP):
                if dy:
                    v = given[dz, NY - dy - 1, j]
                else:
                    v = shards[dz][tab_s[1, o * 8 + j]]
                part = jnp.dot(unpack(v), images[tab_s[0, o * 8 + j]], preferred_element_type=jnp.float32)
                part = part * m[j : j + 1, :]
                total = part if total is None else total + part
            i = dz * NY + dy
            terms[i] = total
            if i:
                send(f"t{i}", terms.at[i], landed.at[i], dev(dzh=dz, dy=dy))

    total = terms[0]
    for dz in (0, 3, 1, 2):
        for dy in (0, 1, 3, 2):
            i = dz * NY + dy
            if i:
                arrive(f"t{i}", landed.at[i])
                total = total + landed[i]
    out[...] = total
    for copy in sent:
        copy.wait_send()


MESSAGES = 3 + 1 + 4 + 4 + 8 + 4 + 12 + 15


def per_device(jacobian, prolong, tile_rows, tile_cols, coarse_slot):
    kt, tile = jacobian.shape[2], jacobian.shape[3]
    vmem = pl.BlockSpec(memory_space=pltpu.VMEM)
    bf = jnp.bfloat16
    result = pl.pallas_call(
        kernel,
        out_shape=jax.ShapeDtypeStruct((64, 128), jnp.float32),
        in_specs=[
            pl.BlockSpec(memory_space=pl.ANY),
            pl.BlockSpec(memory_space=pl.ANY),
            vmem,
            vmem,
            pl.BlockSpec(memory_space=pltpu.SMEM),
        ],
        out_specs=vmem,
        scratch_shapes=[
            pltpu.VMEM((kt, tile, tile), bf),
            pltpu.VMEM((FB, 64, tile), bf),
            pltpu.VMEM((16 * FB, PR, PC), bf),
            pltpu.VMEM((FB, PR, PC), bf),
            pltpu.VMEM((FB, PR, PC), bf),
            pltpu.VMEM((FB, PR, PC), bf),
            pltpu.VMEM((FB, PR, PC), bf),
            pltpu.VMEM((NZH, NY - 1, CAP, PR, PC), bf),
            pltpu.VMEM((NZH, NY - 1, CAP, PR, PC), bf),
            pltpu.VMEM((kt, tile, 128), bf),
            pltpu.VMEM((16, 64, 128), jnp.float32),
            pltpu.VMEM((16, 64, 128), jnp.float32),
            pltpu.VMEM((8, 128), jnp.int32),
            pltpu.SMEM((8, 128), jnp.int32),
            pltpu.VMEM((NY - 1, 8, 128), jnp.int32),
            pltpu.SMEM((NY - 1, 8, 128), jnp.int32),
            pltpu.VMEM((128, 128), jnp.float32),
            pltpu.SemaphoreType.DMA((3,)),
            pltpu.SemaphoreType.DMA((NY - 1,)),
            pltpu.SemaphoreType.DMA((MESSAGES,)),
            pltpu.SemaphoreType.DMA((MESSAGES,)),
        ],
        compiler_params=pltpu.CompilerParams(
            collective_id=0, has_side_effects=True, vmem_limit_bytes=56 * 2**20
        ),
        name="coarse_operator",
    )(
        jacobian.reshape(kt, tile, tile),
        prolong,
        tile_rows.reshape(1, kt),
        coarse_slot.reshape(1, kt),
        tile_cols.reshape(1, kt),
    )
    return result.reshape(1, 1, 64, 128)


def solution(mesh):
    placed = (
        P("row", "col", None, None, None),
        P(("row", "col"), None, None),
        P("row", "col", None),
        P("row", "col", None),
        P("row", "col", None),
    )
    return jax.shard_map(
        per_device,
        mesh=mesh,
        in_specs=placed,
        out_specs=P("row", "col", None, None),
        check_vma=False,
    )
```

time: 269 us -> 77.3 us (0.29)
  the two profiles are of different devices: /device:TPU:1 before, /device:TPU:2 now
where the time goes in v1:
time: 77.3 us; the launch traced here: 77.1 us
  Pallas kernels  75.7 us (98%)
  local copies, waits for them, and re-layouts  1.38 us (2%)
    pallas_call x1, Pallas kernels, per_device(): pl.pallas_call(kernel, out_shape=jax.ShapeDtypeStruct((64, 128), jnp.floa...  75.7 us

profile of v1, /device:TPU:2, one launch (start us, length us, event | category | flops | bytes accessed | tf_op | source)
XLA Modules:
  0.0 77.1 jit_solution(14425982151362881183)
XLA Ops:
  0.0 75.7 %coarse_operator.1 = f32[64,128]{1,0:T(8,128)} custom-call(bf16[56,320,320]{2,1,0:T(8,128)(2,1)} %bitcast.5, bf16[8,64,320]{2,1,0:T(8,128)(2,1)} %pro.1, s32[1,56]{1,0:T(1,128)} %bitcast.7, s32[1,56]{1,0:T(1,128)} %bitcast.8, s32[1,56]{1,0:T(1,128)} %bitcast.9), custom_call_target="tpu_custom_call" | custom-call | tf_op jit(solution)/shard_map/coarse_operator/pallas_call | solution.py:250
  75.7 1.4 %copy.7 = f32[1,1,64,128]{3,2,1,0:T(8,128)} copy(f32[1,1,64,128]{3,2,1,0:T(8,128)} %bitcast.6) | data formatting | bytes 65536

commit v2 on v1

--- a/solution.py
+++ b/solution.py
@@ -13,6 +13,7 @@
 CAP = 5
 PR, PC = 80, 256
 HALF = FB // 2
+CUT = ((0, 48), (48, 32))
 
 
 def pack(p):
@@ -30,7 +31,7 @@
 
 def kernel(
     jac, pro, rows, slots, cols, out,
-    tiles, shard_in, colbuf, own, zm, zp, z2, picked, given, images, terms, landed,
+    tiles, shard_in, colbuf, own, zm0, zm1, zp0, zp1, z2, picked, given, images, terms, landed,
     tab, tab_s, asked, asked_s, mask, local_sem, ask_sem, ss, rs,
 ):
     kt = tiles.shape[0]
@@ -79,7 +80,7 @@
 
     bar = pltpu.get_barrier_semaphore()
     peers = [dev(dc=1), dev(dzl=1), dev(dx=1), dev(dx=3)]
-    peers += [dev(dzh=a, dy=b) for a in range(NZH) for b in range(NY) if (a, b) != (0, 0)]
+    peers += [dev(dzh=a, dy=b) for a in range(NZH) for b in range(NY) if (a, b) in ((0,1),(0,2),(0,3),(1,0),(3,0))]
     for peer in peers:
         pl.semaphore_signal(bar, inc=1, device_id=peer, device_id_type=MESH)
 
@@ -122,11 +123,17 @@
 
     for dy in range(1, NY):
         send(f"ask{dy}", tab, asked.at[dy - 1], dev(dy=dy))
-    send("zl", own, slot_of(mine), dev(dzl=1))
+    zms, zps = (zm0, zm1), (zp0, zp1)
+
+    def lend(ch):
+        first, n = CUT[ch]
+        part = own.at[:, pl.ds(first, n)]
+        send(f"zp{ch}", part, zms[ch], dev(dzh=1))
+        send(f"zm{ch}", part, zps[ch], dev(dzh=3))
+
+    lend(0)
     send("xp", own, slot_of(mine), dev(dx=1))
     send("xm", own, slot_of(mine), dev(dx=3))
-    send("zp", own, zm, dev(dzh=1))
-    send("zm", own, zp, dev(dzh=3))
     send("sib", own, slot_of(mine), dev(dc=1))
 
     put_tab.wait()
@@ -139,15 +146,50 @@
     for copy in asks:
         copy.wait()
 
-    def hand_out(dz, shard):
+    def hand_out(dz, shard, first=0, n=PR):
         owner = ((zh + dz) % NZH) * NY + y
+        rows_of = pl.ds(first, n)
         for d in (1, 3, 2):
             to = NY - d
             for j in range(CAP):
-                picked[dz, to - 1, j] = shard[asked_s[d - 1, 1, owner * 8 + j]]
-            send(f"y{dz}{to}", picked.at[dz, to - 1], given.at[dz, to - 1], dev(dy=to))
+                picked[dz, to - 1, j, rows_of] = shard[asked_s[d - 1, 1, owner * 8 + j]]
+            send(
+                f"y{dz}{to}{first}",
+                picked.at[dz, to - 1, :, rows_of],
+                given.at[dz, to - 1, :, rows_of],
+                dev(dy=to),
+            )
 
     hand_out(0, own)
+
+    def borrow(ch):
+        arrive(f"zp{ch}", zms[ch])
+        arrive(f"zm{ch}", zps[ch])
+
+    def pass_on(ch):
+        at = pl.ds(*CUT[ch])
+        send(f"zpp{ch}", zms[ch].at[pl.ds(0, HALF)], z2.at[pl.ds(0, HALF), at], dev(dzh=1))
+        send(f"zmm{ch}", zps[ch].at[pl.ds(HALF, HALF)], z2.at[pl.ds(HALF, HALF), at], dev(dzh=3))
+
+    def hand_on(ch):
+        hand_out(3, zms[ch], *CUT[ch])
+        hand_out(1, zps[ch], *CUT[ch])
+
+    def get_far():
+        for ch in (0, 1):
+            at = pl.ds(*CUT[ch])
+            arrive(f"zpp{ch}", z2.at[pl.ds(0, HALF), at])
+            arrive(f"zmm{ch}", z2.at[pl.ds(HALF, HALF), at])
+
+    def get_zl():
+        at = held(dzl=1)
+        arrive("zl", slot_of(at))
+        send("xp1", slot_of(at), slot_of(at), dev(dx=1))
+        send("xm1", slot_of(at), slot_of(at), dev(dx=3))
+        send("szl", slot_of(at), slot_of(at), dev(dc=1))
+
+    def put_zl():
+        send("zl", own, slot_of(mine), dev(dzl=1))
 
     def across(tag, dzl):
         at = held(dx=3, dzl=dzl)
@@ -165,27 +207,21 @@
         arrive(f"xmm{tag}", slot_of(at, HALF, HALF))
         send(f"sx2{tag}", slot_of(at), slot_of(at), dev(dc=1))
 
+    put_zl()
+    borrow(0)
+    hand_on(0)
     across("", 0)
-    at = held(dzl=1)
-    arrive("zl", slot_of(at))
-    send("xp1", slot_of(at), slot_of(at), dev(dx=1))
-    send("xm1", slot_of(at), slot_of(at), dev(dx=3))
-    send("szl", slot_of(at), slot_of(at), dev(dc=1))
+    get_zl()
+    lend(1)
+    pass_on(0)
     beyond("", 0)
-
-    arrive("zp", zm)
-    send("zpp", zm.at[pl.ds(0, HALF)], z2.at[pl.ds(0, HALF)], dev(dzh=1))
-    arrive("zm", zp)
-    send("zmm", zp.at[pl.ds(HALF, HALF)], z2.at[pl.ds(HALF, HALF)], dev(dzh=3))
-    hand_out(3, zm)
-    hand_out(1, zp)
-
+    borrow(1)
+    pass_on(1)
+    hand_on(1)
     across("1", 1)
-    arrive("zpp", z2.at[pl.ds(0, HALF)])
-    arrive("zmm", z2.at[pl.ds(HALF, HALF)])
+    get_far()
     hand_out(2, z2)
     beyond("1", 1)
-
     at = held(dc=1)
     arrive("sib", slot_of(at))
     for tag, dzl in (("", 0), ("1", 1)):
@@ -204,43 +240,49 @@
         ).astype(jnp.bfloat16)
         return carry
 
-    lax.fori_loop(0, kt, image, 0, unroll=2)
-
-    shards = {0: own, 1: zp, 2: z2, 3: zm}
+    lax.fori_loop(0, kt, image, 0, unroll=14)
+
+    def kept(dz, b):
+        if dz in (1, 3):
+            return jnp.concatenate([part[b] for part in (zps if dz == 1 else zms)], axis=0)
+        return (z2 if dz else own)[b]
+
     here = None
     for dz in (0, 3, 1, 2):
         for dy in (0, 1, 3, 2):
             o = ((zh + dz) % NZH) * NY + (y + dy) % NY
             if dy:
-                arrive(f"y{dz}{NY - dy}", given.at[dz, NY - dy - 1])
+                for first, n in CUT if dz in (1, 3) else ((0, PR),):
+                    arrive(f"y{dz}{NY - dy}{first}", given.at[dz, NY - dy - 1, :, pl.ds(first, n)])
             m = mask[pl.ds(pl.multiple_of(o * 8, 8), 8), :]
             total = None
             for j in range(CAP):
                 if dy:
                     v = given[dz, NY - dy - 1, j]
                 else:
-                    v = shards[dz][tab_s[1, o * 8 + j]]
+                    v = kept(dz, tab_s[1, o * 8 + j])
                 part = jnp.dot(unpack(v), images[tab_s[0, o * 8 + j]], preferred_element_type=jnp.float32)
                 part = part * m[j : j + 1, :]
                 total = part if total is None else total + part
             i = dz * NY + dy
-            terms[i] = total
+            terms[i] = total.astype(jnp.bfloat16)
+            if not i: here = total
             if i:
                 send(f"t{i}", terms.at[i], landed.at[i], dev(dzh=dz, dy=dy))
 
-    total = terms[0]
+    total = here
     for dz in (0, 3, 1, 2):
         for dy in (0, 1, 3, 2):
             i = dz * NY + dy
             if i:
                 arrive(f"t{i}", landed.at[i])
-                total = total + landed[i]
+                total = total + landed[i].astype(jnp.float32)
     out[...] = total
     for copy in sent:
         copy.wait_send()
 
 
-MESSAGES = 3 + 1 + 4 + 4 + 8 + 4 + 12 + 15
+MESSAGES = 3 + 1 + 4 + 8 + 8 + 4 + 18 + 15
 
 
 def per_device(jacobian, prolong, tile_rows, tile_cols, coarse_slot):
@@ -263,14 +305,16 @@
             pltpu.VMEM((FB, 64, tile), bf),
             pltpu.VMEM((16 * FB, PR, PC), bf),
             pltpu.VMEM((FB, PR, PC), bf),
-            pltpu.VMEM((FB, PR, PC), bf),
-            pltpu.VMEM((FB, PR, PC), bf),
+            pltpu.VMEM((FB, CUT[0][1], PC), bf),
+            pltpu.VMEM((FB, CUT[1][1], PC), bf),
+            pltpu.VMEM((FB, CUT[0][1], PC), bf),
+            pltpu.VMEM((FB, CUT[1][1], PC), bf),
             pltpu.VMEM((FB, PR, PC), bf),
             pltpu.VMEM((NZH, NY - 1, CAP, PR, PC), bf),
             pltpu.VMEM((NZH, NY - 1, CAP, PR, PC), bf),
             pltpu.VMEM((kt, tile, 128), bf),
-            pltpu.VMEM((16, 64, 128), jnp.float32),
-            pltpu.VMEM((16, 64, 128), jnp.float32),
+            pltpu.VMEM((16, 64, 128), bf),
+            pltpu.VMEM((16, 64, 128), bf),
             pltpu.VMEM((8, 128), jnp.int32),
             pltpu.SMEM((8, 128), jnp.int32),
             pltpu.VMEM((NY - 1, 8, 128), jnp.int32),

time: 77.3 us -> 63.3 us (0.82)
  the two profiles are of different devices: /device:TPU:2 before, /device:TPU:1 now
where the time goes in v2:
time: 63.3 us; the launch traced here: 63.2 us
  Pallas kernels  61.8 us (98%)
  local copies, waits for them, and re-layouts  1.38 us (2%)
    pallas_call x1, Pallas kernels, per_device(): pl.pallas_call(kernel, out_shape=jax.ShapeDtypeStruct((64, 128), jnp.floa...  61.8 us
    unnamed x1, local copies, waits for them, and re-layouts  1.38 us

profile of v2, /device:TPU:1, one launch (start us, length us, event | category | flops | bytes accessed | tf_op | source)
XLA Modules:
  0.0 63.2 jit_solution(16771041118551730241)
XLA Ops:
  0.0 61.8 %coarse_operator.1 = f32[64,128]{1,0:T(8,128)} custom-call(bf16[56,320,320]{2,1,0:T(8,128)(2,1)} %bitcast.5, bf16[8,64,320]{2,1,0:T(8,128)(2,1)} %pro.1, s32[1,56]{1,0:T(1,128)} %bitcast.7, s32[1,56]{1,0:T(1,128)} %bitcast.8, s32[1,56]{1,0:T(1,128)} %bitcast.9), custom_call_target="tpu_custom_call" | custom-call | tf_op jit(solution)/shard_map/coarse_operator/pallas_call | solution.py:292
  61.8 1.4 %copy.7 = f32[1,1,64,128]{3,2,1,0:T(8,128)} copy(f32[1,1,64,128]{3,2,1,0:T(8,128)} %bitcast.6) | data formatting | bytes 65536

commit v3 on v2

--- a/solution.py
+++ b/solution.py
@@ -13,7 +13,7 @@
 CAP = 5
 PR, PC = 80, 256
 HALF = FB // 2
-CUT = ((0, 48), (48, 32))
+CUT = ((0, 64), (64, 16))
 
 
 def pack(p):
@@ -40,14 +40,17 @@
     x, zl, c = r // 4, (r // 2) % 2, r % 2
     zh, y = q // NY, q % NY
 
+    xs = [(x + d) % NX for d in range(NX)]
+    zls = [zl, 1 - zl]
+    cs = [c, 1 - c]
+    zhs = [(zh + d) % NZH for d in range(NZH)]
+    ys = [(y + d) % NY for d in range(NY)]
+
     def dev(dx=0, dzl=0, dc=0, dzh=0, dy=0):
-        return (
-            ((x + dx) % NX) * 4 + ((zl + dzl) % NZL) * 2 + (c + dc) % NC,
-            ((zh + dzh) % NZH) * NY + (y + dy) % NY,
-        )
+        return xs[dx] * 4 + zls[dzl] * 2 + cs[dc], zhs[dzh] * NY + ys[dy]
 
     def held(dx=0, dzl=0, dc=0):
-        return (((x + dx) % NX) * 4 + ((zl + dzl) % NZL) * 2 + (c + dc) % NC) * FB
+        return (xs[dx] * 4 + zls[dzl] * 2 + cs[dc]) * FB
 
     sent = []
     count = [0]
@@ -147,7 +150,7 @@
         copy.wait()
 
     def hand_out(dz, shard, first=0, n=PR):
-        owner = ((zh + dz) % NZH) * NY + y
+        owner = zhs[dz] * NY + y
         rows_of = pl.ds(first, n)
         for d in (1, 3, 2):
             to = NY - d
@@ -240,7 +243,7 @@
         ).astype(jnp.bfloat16)
         return carry
 
-    lax.fori_loop(0, kt, image, 0, unroll=14)
+    lax.fori_loop(0, kt, image, 0, unroll=28)
 
     def kept(dz, b):
         if dz in (1, 3):
@@ -248,9 +251,9 @@
         return (z2 if dz else own)[b]
 
     here = None
-    for dz in (0, 3, 1, 2):
-        for dy in (0, 1, 3, 2):
-            o = ((zh + dz) % NZH) * NY + (y + dy) % NY
+    turns = [(dz, 0) for dz in (2, 3, 1, 0)] + [(dz, dy) for dz in (0, 3, 1, 2) for dy in (2, 1, 3)]
+    for dz, dy in turns:
+            o = zhs[dz] * NY + ys[dy]
             if dy:
                 for first, n in CUT if dz in (1, 3) else ((0, PR),):
                     arrive(f"y{dz}{NY - dy}{first}", given.at[dz, NY - dy - 1, :, pl.ds(first, n)])

time: 63.3 us -> 61.5 us (0.972)
  Pallas kernels: 61.8 us -> 59.9 us
    pallas_call x1, Pallas kernels: 61.8 us -> 59.9 us  [per_device(): pl.pallas_call(kernel, out_shape=jax.ShapeDtypeStruct((64, 128), jnp.floa...]
where the time goes in v3:
time: 61.5 us; the launch traced here: 61.3 us
  Pallas kernels  59.9 us (97%)
  local copies, waits for them, and re-layouts  1.38 us (2%)
    pallas_call x1, Pallas kernels, per_device(): pl.pallas_call(kernel, out_shape=jax.ShapeDtypeStruct((64, 128), jnp.floa...  59.9 us
    unnamed x1, local copies, waits for them, and re-layouts  1.38 us

profile of v3, /device:TPU:1, one launch (start us, length us, event | category | flops | bytes accessed | tf_op | source)
XLA Modules:
  0.0 61.3 jit_solution(14738542795973508634)
XLA Ops:
  0.0 59.9 %coarse_operator.1 = f32[64,128]{1,0:T(8,128)} custom-call(bf16[56,320,320]{2,1,0:T(8,128)(2,1)} %bitcast.5, bf16[8,64,320]{2,1,0:T(8,128)(2,1)} %pro.1, s32[1,56]{1,0:T(1,128)} %bitcast.7, s32[1,56]{1,0:T(1,128)} %bitcast.8, s32[1,56]{1,0:T(1,128)} %bitcast.9), custom_call_target="tpu_custom_call" | custom-call | tf_op jit(solution)/shard_map/coarse_operator/pallas_call | solution.py:295
  59.9 1.4 %copy.7 = f32[1,1,64,128]{3,2,1,0:T(8,128)} copy(f32[1,1,64,128]{3,2,1,0:T(8,128)} %bitcast.6) | data formatting | bytes 65536

commit v4 on v3

--- a/solution.py
+++ b/solution.py
@@ -13,7 +13,8 @@
 CAP = 5
 PR, PC = 80, 256
 HALF = FB // 2
-CUT = ((0, 64), (64, 16))
+CUT = ((0, 48), (48, 32))
+EARLY = 32
 
 
 def pack(p):
@@ -31,7 +32,7 @@
 
 def kernel(
     jac, pro, rows, slots, cols, out,
-    tiles, shard_in, colbuf, own, zm0, zm1, zp0, zp1, z2, picked, given, images, terms, landed,
+    tiles, shard_in, colbuf, own, zm0, zm1, zp0, zp1, z20, z21, ahead, picked, given, images, terms, landed,
     tab, tab_s, asked, asked_s, mask, local_sem, ask_sem, ss, rs,
 ):
     kt = tiles.shape[0]
@@ -126,7 +127,7 @@
 
     for dy in range(1, NY):
         send(f"ask{dy}", tab, asked.at[dy - 1], dev(dy=dy))
-    zms, zps = (zm0, zm1), (zp0, zp1)
+    zms, zps, z2s = (zm0, zm1), (zp0, zp1), (z20, z21)
 
     def lend(ch):
         first, n = CUT[ch]
@@ -134,6 +135,8 @@
         send(f"zp{ch}", part, zms[ch], dev(dzh=1))
         send(f"zm{ch}", part, zps[ch], dev(dzh=3))
 
+    for dy in (2, 1, 3):
+        send(f"e{dy}", own.at[:, pl.ds(0, EARLY)], ahead.at[dy - 1], dev(dy=dy))
     lend(0)
     send("xp", own, slot_of(mine), dev(dx=1))
     send("xm", own, slot_of(mine), dev(dx=3))
@@ -163,26 +166,25 @@
                 dev(dy=to),
             )
 
-    hand_out(0, own)
+    hand_out(0, own.at[:, pl.ds(EARLY, PR - EARLY)], EARLY, PR - EARLY)
 
     def borrow(ch):
         arrive(f"zp{ch}", zms[ch])
         arrive(f"zm{ch}", zps[ch])
 
     def pass_on(ch):
-        at = pl.ds(*CUT[ch])
-        send(f"zpp{ch}", zms[ch].at[pl.ds(0, HALF)], z2.at[pl.ds(0, HALF), at], dev(dzh=1))
-        send(f"zmm{ch}", zps[ch].at[pl.ds(HALF, HALF)], z2.at[pl.ds(HALF, HALF), at], dev(dzh=3))
+        far = z2s[ch]
+        send(f"zpp{ch}", zms[ch].at[pl.ds(0, HALF)], far.at[pl.ds(0, HALF)], dev(dzh=1))
+        send(f"zmm{ch}", zps[ch].at[pl.ds(HALF, HALF)], far.at[pl.ds(HALF, HALF)], dev(dzh=3))
 
     def hand_on(ch):
         hand_out(3, zms[ch], *CUT[ch])
         hand_out(1, zps[ch], *CUT[ch])
 
-    def get_far():
-        for ch in (0, 1):
-            at = pl.ds(*CUT[ch])
-            arrive(f"zpp{ch}", z2.at[pl.ds(0, HALF), at])
-            arrive(f"zmm{ch}", z2.at[pl.ds(HALF, HALF), at])
+    def get_far(ch):
+        arrive(f"zpp{ch}", z2s[ch].at[pl.ds(0, HALF)])
+        arrive(f"zmm{ch}", z2s[ch].at[pl.ds(HALF, HALF)])
+        hand_out(2, z2s[ch], *CUT[ch])
 
     def get_zl():
         at = held(dzl=1)
@@ -222,8 +224,8 @@
     pass_on(1)
     hand_on(1)
     across("1", 1)
-    get_far()
-    hand_out(2, z2)
+    get_far(0)
+    get_far(1)
     beyond("1", 1)
     at = held(dc=1)
     arrive("sib", slot_of(at))
@@ -246,22 +248,27 @@
     lax.fori_loop(0, kt, image, 0, unroll=28)
 
     def kept(dz, b):
-        if dz in (1, 3):
-            return jnp.concatenate([part[b] for part in (zps if dz == 1 else zms)], axis=0)
-        return (z2 if dz else own)[b]
+        if dz:
+            return jnp.concatenate([part[b] for part in (None, zps, z2s, zms)[dz]], axis=0)
+        return own[b]
 
     here = None
+    for dy in range(1, NY):
+        arrive(f"e{dy}", ahead.at[dy - 1])
     turns = [(dz, 0) for dz in (2, 3, 1, 0)] + [(dz, dy) for dz in (0, 3, 1, 2) for dy in (2, 1, 3)]
     for dz, dy in turns:
             o = zhs[dz] * NY + ys[dy]
             if dy:
-                for first, n in CUT if dz in (1, 3) else ((0, PR),):
+                for first, n in {0: ((EARLY, PR - EARLY),)}.get(dz, CUT):
                     arrive(f"y{dz}{NY - dy}{first}", given.at[dz, NY - dy - 1, :, pl.ds(first, n)])
             m = mask[pl.ds(pl.multiple_of(o * 8, 8), 8), :]
             total = None
             for j in range(CAP):
                 if dy:
                     v = given[dz, NY - dy - 1, j]
+                    if not dz:
+                        first = ahead[NY - dy - 1, tab_s[1, o * 8 + j]]
+                        v = jnp.concatenate([first, v[EARLY:]], axis=0)
                 else:
                     v = kept(dz, tab_s[1, o * 8 + j])
                 part = jnp.dot(unpack(v), images[tab_s[0, o * 8 + j]], preferred_element_type=jnp.float32)
@@ -285,7 +292,7 @@
         copy.wait_send()
 
 
-MESSAGES = 3 + 1 + 4 + 8 + 8 + 4 + 18 + 15
+MESSAGES = 3 + 3 + 1 + 4 + 8 + 8 + 4 + 21 + 15
 
 
 def per_device(jacobian, prolong, tile_rows, tile_cols, coarse_slot):
@@ -312,7 +319,9 @@
             pltpu.VMEM((FB, CUT[1][1], PC), bf),
             pltpu.VMEM((FB, CUT[0][1], PC), bf),
             pltpu.VMEM((FB, CUT[1][1], PC), bf),
-            pltpu.VMEM((FB, PR, PC), bf),
+            pltpu.VMEM((FB, CUT[0][1], PC), bf),
+            pltpu.VMEM((FB, CUT[1][1], PC), bf),
+            pltpu.VMEM((NY - 1, FB, EARLY, PC), bf),
             pltpu.VMEM((NZH, NY - 1, CAP, PR, PC), bf),
             pltpu.VMEM((NZH, NY - 1, CAP, PR, PC), bf),
             pltpu.VMEM((kt, tile, 128), bf),

time: 61.5 us -> 61.7 us (level)
  no operation moved by 1% of the time
where the time goes in v4:
time: 61.7 us; the launch traced here: 61.6 us
  Pallas kernels  60.2 us (98%)
  local copies, waits for them, and re-layouts  1.38 us (2%)
    pallas_call x1, Pallas kernels, per_device(): pl.pallas_call(kernel, out_shape=jax.ShapeDtypeStruct((64, 128), jnp.floa...  60.2 us
    unnamed x1, local copies, waits for them, and re-layouts  1.38 us

profile of v4, /device:TPU:1, one launch (start us, length us, event | category | flops | bytes accessed | tf_op | source)
XLA Modules:
  0.0 61.6 jit_solution(785690397934117039)
XLA Ops:
  0.0 60.2 %coarse_operator.1 = f32[64,128]{1,0:T(8,128)} custom-call(bf16[56,320,320]{2,1,0:T(8,128)(2,1)} %bitcast.5, bf16[8,64,320]{2,1,0:T(8,128)(2,1)} %pro.1, s32[1,56]{1,0:T(1,128)} %bitcast.7, s32[1,56]{1,0:T(1,128)} %bitcast.8, s32[1,56]{1,0:T(1,128)} %bitcast.9), custom_call_target="tpu_custom_call" | custom-call | tf_op jit(solution)/shard_map/coarse_operator/pallas_call | solution.py:302
  60.2 1.4 %copy.7 = f32[1,1,64,128]{3,2,1,0:T(8,128)} copy(f32[1,1,64,128]{3,2,1,0:T(8,128)} %bitcast.6) | data formatting | bytes 65536
